TPU v7x, 512 devices: a whole 4x4x16 slice. The times are simulated.
512 devices in a mesh: ctx: 16 (over z), head: 8 (over x, y_hi), pack: 4 (over y_lo, core).
Axes of the slice: x: 4, y: 4 (y_hi: 2, y_lo: 2; y = y_hi * 2 + y_lo), z: 16, core: 2. Of those that a mesh axis runs over, the one named last changes fastest.
Arguments:
- queries: bfloat16 [2048, 16384], P(('pack', 'ctx'), 'head'), parts along dimension 0, may hold values from -12 to 12
- cached_keys: bfloat16 [65536, 1024], P(('pack', 'ctx'), 'head'), parts along dimension 0, may hold values from -6 to 6
- cached_values: bfloat16 [65536, 1024], P(('pack', 'ctx'), 'head'), parts along dimension 0, may hold values from -15 to 15
- turn_lengths: int32 [32], P('pack'), parts along dimension 0, may hold values from 1 to 128, 512 in all
- tile_map: int32 [32, 16], P('pack'), parts along dimension 0, may hold values from 0 to 1, as said below
- prefix_len: int32 [64], P('pack'), parts along dimension 0, may hold values from 2 to 1024, as said below
- owner_ids: int32 [64], P('pack'), parts along dimension 0, may hold values from 0 to 15, each once
Outputs:
- attended: bfloat16 [2048, 16384], P(('pack', 'ctx'), 'head'), parts along dimension 0
There are 4 independent parts, one for each index of `pack`. A program takes and returns all parts, laid end to end along the dimension named above; each array names one. Nothing has to cross between parts.
Inputs may be any that keep to these rules, and one draw needn't show every extreme that they name: `turn_lengths`: every turn is 1 row or more and they sum to 512. `tile_map`: every turn sees at least one cache shard. `prefix_len`: some shard is full. `owner_ids`: a permutation of 0..15.
All inputs are finite; a program needn't handle non-finite values.
Results may differ from a plain program's by a relative error of at most 0.0052.
Values may be sent and summed in bfloat16 or wider, within the bound.
A program may use at most 64 MiB of HBM per device.

v0:
```python
import jax
import jax.numpy as jnp
from jax import lax
from jax.sharding import PartitionSpec as P

HD = 128


NEG = -1e30


def passed_along(x, axis, by):
    length = lax.axis_size(axis)
    return lax.ppermute(x, axis, [(i, (i + by) % length) for i in range(length)])


def select_entry(table, position):
    hits = lax.broadcasted_iota(jnp.int32, table.shape, table.ndim - 1) == position
    return jnp.sum(jnp.where(hits, table, 0), axis=table.ndim - 1)


def shard_partial(block, keys, values, row_seen, key_live):
    rows = block.shape[0]
    groups = keys.shape[1] // HD
    query = block.reshape(rows, groups, -1, HD)
    key_tiles = keys.reshape(keys.shape[0], groups, HD)
    value_tiles = values.reshape(values.shape[0], groups, HD)
    scores = jnp.einsum(
        "qgjd,kgd->gjqk", query, key_tiles, preferred_element_type=jnp.float32
    ) * HD ** (-0.5)
    mask = row_seen[None, None, :, None] & key_live[None, None, None, :]
    peak = jnp.max(jnp.where(mask, scores, NEG), axis=3)
    weights = jnp.where(mask, jnp.exp(scores - peak[..., None]), 0.0)
    total = jnp.maximum(jnp.sum(weights, axis=3), 1.0)
    mixed = jnp.einsum(
        "gjqk,kgd->qgjd",
        weights.astype(jnp.bfloat16),
        value_tiles,
        preferred_element_type=jnp.float32,
    )
    mixed = (
        (mixed / jnp.transpose(total, (2, 0, 1))[..., None]).astype(jnp.bfloat16).reshape(rows, -1)
    )
    spread = jnp.transpose(peak + jnp.log(total), (2, 0, 1)).reshape(rows, -1)
    return (mixed, spread)


def per_device(queries, cached_keys, cached_values, turn_lengths, tile_map, prefix_len, owner_ids):
    index = lax.axis_index("ctx")
    count = lax.axis_size("ctx")
    rows = queries.shape[0]
    width = queries.shape[1]
    heads = width // HD
    shard_rows = cached_keys.shape[0]
    ends = jnp.cumsum(turn_lengths)
    turn_ids = lax.iota(jnp.int32, turn_lengths.shape[0])
    slot_ids = lax.iota(jnp.int32, count)
    inverse = jnp.sum(
        jnp.where(owner_ids[None, :] == slot_ids[:, None], slot_ids[None, :], 0), axis=1
    )

    def tile_partial(block, block_index, shard, keys, values):
        positions = block_index * rows + lax.iota(jnp.int32, rows)
        turns = jnp.sum((positions[:, None] >= ends[None, :]).astype(jnp.int32), axis=1)
        column = select_entry(tile_map, shard)
        row_seen = (
            jnp.sum(jnp.where(turns[:, None] == turn_ids[None, :], column[None, :], 0), axis=1) > 0
        )
        limit = select_entry(prefix_len, shard)
        key_live = lax.iota(jnp.int32, shard_rows) < limit
        return shard_partial(block, keys, values, row_seen, key_live)

    def visit(block, source, outputs):
        mixed, spread = tile_partial(block, source, index, cached_keys, cached_values)
        return (
            lax.dynamic_update_index_in_dim(outputs[0], mixed, source, 0),
            lax.dynamic_update_index_in_dim(outputs[1], spread, source, 0),
        )

    def move_up(block):
        return passed_along(block, "ctx", 1)

    outputs = (
        jnp.zeros((count, rows, width), jnp.bfloat16),
        jnp.zeros((count, rows, heads), jnp.float32),
    )
    outputs = visit(queries, index, outputs)

    def advance(step, carry):
        block, gathered = carry
        block = move_up(block)
        return (block, visit(block, (index - step) % count, gathered))

    _, outputs = lax.fori_loop(1, count, advance, (queries, outputs))
    routed = (jnp.take(outputs[0], inverse, axis=0), jnp.take(outputs[1], inverse, axis=0))
    mixed = lax.all_to_all(
        routed[0].astype(jnp.float32), "ctx", split_axis=0, concat_axis=0, tiled=True
    ).astype(jnp.bfloat16)
    spread = lax.all_to_all(routed[1], "ctx", split_axis=0, concat_axis=0, tiled=True)
    sources = spread.shape[0]
    items = spread.shape[1]
    top = jnp.max(spread, axis=0)
    factor = jnp.exp(spread - top[None])
    total = jnp.sum(factor, axis=0)
    merged = jnp.sum(factor[..., None] * mixed.reshape(sources, items, heads, HD), axis=0)
    return (merged / total[..., None]).reshape(items, width).astype(jnp.bfloat16)


def solution(mesh):
    return jax.shard_map(
        per_device,
        mesh=mesh,
        in_specs=(
            P(("pack", "ctx"), "head"),
            P(("pack", "ctx"), "head"),
            P(("pack", "ctx"), "head"),
            P("pack"),
            P("pack", None),
            P("pack"),
            P("pack"),
        ),
        out_specs=P(("pack", "ctx"), "head"),
        check_vma=False,
    )
```

profile of v0, /device:TPU:24, one launch (start us, length us, event | category | flops | bytes accessed | tf_op | source)
XLA Modules:
  0.0 277.6 jit_solution(3040925688498863189)
XLA Ops:
  0.0 0.9 copy.64
  0.9 0.8 select_reduce_fusion.3
  1.7 0.8 reduce-window.8
  2.6 0.8 select_reduce_fusion.5
  3.5 1.3 select_reduce_fusion.6
  5.5 1.5 fusion.22
  9.2 158.6 %while.20 = (s32[]{:T(128)}, bf16[32,2048]{1,0:T(8,128)(2,1)S(1)}, bf16[16,32,2048]{2,1,0:T(8,128)(2,1)S(1)}, f32[16,32,16]{1,2,0:T(8,128)S(1)}, s32[]{:T(128)},...) while((s32[]{:T(128)}, bf16[32,2048]{1,0:T(8,128)(2,1)S(1)}, ...), condition=%wide.region_15.16_spmd.clone, body=%wide.region_8.15_spmd.clone.sunk | while | flops 274369856 | bytes 8824696 | solution.py:94
  9.2 3.8 %collective-permute-start = (bf16[32,2048]{1,0:T(8,128)(2,1)S(1)}, bf16[32,2048]{1,0:T(8,128)(2,1)S(1)}, u32[]{:S(2)}, u32[]{:S(2)}) collective-permute-start(bf16[32,2048]{1,0:T(8,128)(2,1)S(1)} %get-tuple-element.402), channel_id=1, source_target_pairs={{0,32},{32,64},{64,96},{96,128},{128,160},{160,192},{192,224},{224... | collective-permute-start | bytes 393224 | tf_op jit(solution)/shard_map/while/body/eval_jaxpr/ppermute | solution.py:14
  14.6 9.4 %collective-permute-done = bf16[32,2048]{1,0:T(8,128)(2,1)S(1)} collective-permute-done((bf16[32,2048]{1,0:T(8,128)(2,1)S(1)}, bf16[32,2048]{1,0:T(8,128)(2,1)S(1)}, u32[]{:S(2)}, u32[]{:S(2)}) %collective-permute-start) | collective-permute-done | bytes 131104 | tf_op jit(solution)/shard_map/while/body/eval_jaxpr/ppermute | solution.py:14
  26.0 1.9 collective-permute-start
  29.5 4.5 %collective-permute-done = bf16[32,2048]{1,0:T(8,128)(2,1)S(1)} collective-permute-done((bf16[32,2048]{1,0:T(8,128)(2,1)S(1)}, bf16[32,2048]{1,0:T(8,128)(2,1)S(1)}, u32[]{:S(2)}, u32[]{:S(2)}) %collective-permute-start) | collective-permute-done | bytes 131104 | tf_op jit(solution)/shard_map/while/body/eval_jaxpr/ppermute | solution.py:14
  36.0 1.9 collective-permute-start
  39.5 4.5 %collective-permute-done = bf16[32,2048]{1,0:T(8,128)(2,1)S(1)} collective-permute-done((bf16[32,2048]{1,0:T(8,128)(2,1)S(1)}, bf16[32,2048]{1,0:T(8,128)(2,1)S(1)}, u32[]{:S(2)}, u32[]{:S(2)}) %collective-permute-start) | collective-permute-done | bytes 131104 | tf_op jit(solution)/shard_map/while/body/eval_jaxpr/ppermute | solution.py:14
  46.0 1.9 collective-permute-start
  49.5 4.5 %collective-permute-done = bf16[32,2048]{1,0:T(8,128)(2,1)S(1)} collective-permute-done((bf16[32,2048]{1,0:T(8,128)(2,1)S(1)}, bf16[32,2048]{1,0:T(8,128)(2,1)S(1)}, u32[]{:S(2)}, u32[]{:S(2)}) %collective-permute-start) | collective-permute-done | bytes 131104 | tf_op jit(solution)/shard_map/while/body/eval_jaxpr/ppermute | solution.py:14
  56.0 1.9 collective-permute-start
  59.5 4.5 %collective-permute-done = bf16[32,2048]{1,0:T(8,128)(2,1)S(1)} collective-permute-done((bf16[32,2048]{1,0:T(8,128)(2,1)S(1)}, bf16[32,2048]{1,0:T(8,128)(2,1)S(1)}, u32[]{:S(2)}, u32[]{:S(2)}) %collective-permute-start) | collective-permute-done | bytes 131104 | tf_op jit(solution)/shard_map/while/body/eval_jaxpr/ppermute | solution.py:14
  66.0 1.9 collective-permute-start
  69.5 4.5 %collective-permute-done = bf16[32,2048]{1,0:T(8,128)(2,1)S(1)} collective-permute-done((bf16[32,2048]{1,0:T(8,128)(2,1)S(1)}, bf16[32,2048]{1,0:T(8,128)(2,1)S(1)}, u32[]{:S(2)}, u32[]{:S(2)}) %collective-permute-start) | collective-permute-done | bytes 131104 | tf_op jit(solution)/shard_map/while/body/eval_jaxpr/ppermute | solution.py:14
  76.0 1.9 collective-permute-start
  79.5 4.5 %collective-permute-done = bf16[32,2048]{1,0:T(8,128)(2,1)S(1)} collective-permute-done((bf16[32,2048]{1,0:T(8,128)(2,1)S(1)}, bf16[32,2048]{1,0:T(8,128)(2,1)S(1)}, u32[]{:S(2)}, u32[]{:S(2)}) %collective-permute-start) | collective-permute-done | bytes 131104 | tf_op jit(solution)/shard_map/while/body/eval_jaxpr/ppermute | solution.py:14
  85.9 1.9 collective-permute-start
  89.5 5.6 %collective-permute-done = bf16[32,2048]{1,0:T(8,128)(2,1)S(1)} collective-permute-done((bf16[32,2048]{1,0:T(8,128)(2,1)S(1)}, bf16[32,2048]{1,0:T(8,128)(2,1)S(1)}, u32[]{:S(2)}, u32[]{:S(2)}) %collective-permute-start) | collective-permute-done | bytes 131104 | tf_op jit(solution)/shard_map/while/body/eval_jaxpr/ppermute | solution.py:14
  97.1 1.9 collective-permute-start
  100.7 5.0 %collective-permute-done = bf16[32,2048]{1,0:T(8,128)(2,1)S(1)} collective-permute-done((bf16[32,2048]{1,0:T(8,128)(2,1)S(1)}, bf16[32,2048]{1,0:T(8,128)(2,1)S(1)}, u32[]{:S(2)}, u32[]{:S(2)}) %collective-permute-start) | collective-permute-done | bytes 131104 | tf_op jit(solution)/shard_map/while/body/eval_jaxpr/ppermute | solution.py:14
  107.6 1.9 collective-permute-start
  111.2 4.5 %collective-permute-done = bf16[32,2048]{1,0:T(8,128)(2,1)S(1)} collective-permute-done((bf16[32,2048]{1,0:T(8,128)(2,1)S(1)}, bf16[32,2048]{1,0:T(8,128)(2,1)S(1)}, u32[]{:S(2)}, u32[]{:S(2)}) %collective-permute-start) | collective-permute-done | bytes 131104 | tf_op jit(solution)/shard_map/while/body/eval_jaxpr/ppermute | solution.py:14
  117.6 1.9 collective-permute-start
  121.2 4.5 %collective-permute-done = bf16[32,2048]{1,0:T(8,128)(2,1)S(1)} collective-permute-done((bf16[32,2048]{1,0:T(8,128)(2,1)S(1)}, bf16[32,2048]{1,0:T(8,128)(2,1)S(1)}, u32[]{:S(2)}, u32[]{:S(2)}) %collective-permute-start) | collective-permute-done | bytes 131104 | tf_op jit(solution)/shard_map/while/body/eval_jaxpr/ppermute | solution.py:14
  127.6 1.9 collective-permute-start
  131.2 4.5 %collective-permute-done = bf16[32,2048]{1,0:T(8,128)(2,1)S(1)} collective-permute-done((bf16[32,2048]{1,0:T(8,128)(2,1)S(1)}, bf16[32,2048]{1,0:T(8,128)(2,1)S(1)}, u32[]{:S(2)}, u32[]{:S(2)}) %collective-permute-start) | collective-permute-done | bytes 131104 | tf_op jit(solution)/shard_map/while/body/eval_jaxpr/ppermute | solution.py:14
  137.6 1.9 collective-permute-start
  141.2 4.5 %collective-permute-done = bf16[32,2048]{1,0:T(8,128)(2,1)S(1)} collective-permute-done((bf16[32,2048]{1,0:T(8,128)(2,1)S(1)}, bf16[32,2048]{1,0:T(8,128)(2,1)S(1)}, u32[]{:S(2)}, u32[]{:S(2)}) %collective-permute-start) | collective-permute-done | bytes 131104 | tf_op jit(solution)/shard_map/while/body/eval_jaxpr/ppermute | solution.py:14
  147.6 1.9 collective-permute-start
  151.2 4.5 %collective-permute-done = bf16[32,2048]{1,0:T(8,128)(2,1)S(1)} collective-permute-done((bf16[32,2048]{1,0:T(8,128)(2,1)S(1)}, bf16[32,2048]{1,0:T(8,128)(2,1)S(1)}, u32[]{:S(2)}, u32[]{:S(2)}) %collective-permute-start) | collective-permute-done | bytes 131104 | tf_op jit(solution)/shard_map/while/body/eval_jaxpr/ppermute | solution.py:14
  157.6 1.9 collective-permute-start
  161.2 4.7 %collective-permute-done = bf16[32,2048]{1,0:T(8,128)(2,1)S(1)} collective-permute-done((bf16[32,2048]{1,0:T(8,128)(2,1)S(1)}, bf16[32,2048]{1,0:T(8,128)(2,1)S(1)}, u32[]{:S(2)}, u32[]{:S(2)}) %collective-permute-start) | collective-permute-done | bytes 131104 | tf_op jit(solution)/shard_map/while/body/eval_jaxpr/ppermute | solution.py:14
  168.4 0.7 reshape.345
  169.2 9.6 %all-to-all-start = ((f32[16,1,512]{2,1,0:T(1,128)}), f32[16,1,512]{2,1,0:T(1,128)S(1)}, u32[]{:S(2)}, u32[]{:S(2)}) async-start(f32[16,1,512]{2,1,0:T(1,128)} %reshape.345), calls=%async_computation | async-start | bytes 65536 | tf_op jit(solution)/shard_map/all_to_all | solution.py:99
  178.8 2.1 gather_fusion.1
  180.9 3.2 %select_convert_fusion = bf16[16,32,2048]{2,1,0:T(8,128)(2,1)} fusion(bf16[16,32,2048]{2,1,0:T(8,128)(2,1)} %gather_fusion.1, pred[16]{0:T(512)(128)(4,1)S(1)} %compare_and_fusion), kind=kLoop, calls=%fused_computation.46 | loop fusion | flops 1048576 | bytes 4194320 | tf_op jit(solution)/shard_map/convert_element_type | solution.py:97
  184.1 10.6 %all-to-all-done = f32[16,1,512]{2,1,0:T(1,128)S(1)} async-done(((f32[16,1,512]{2,1,0:T(1,128)}), f32[16,1,512]{2,1,0:T(1,128)S(1)}, u32[]{:S(2)}, u32[]{:S(2)}) %all-to-all-start) | async-done | bytes 32800 | tf_op jit(solution)/shard_map/all_to_all | solution.py:99
  194.7 9.4 %all-to-all-start.1 = ((bf16[16,32,2048]{2,1,0:T(8,128)(2,1)}), bf16[16,32,2048]{2,1,0:T(8,128)(2,1)S(1)}, u32[]{:S(2)}, u32[]{:S(2)}) async-start(bf16[16,32,2048]{2,1,0:T(8,128)(2,1)} %select_convert_fusion), calls=%async_computation.1 | async-start | bytes 4194304 | tf_op jit(solution)/shard_map/all_to_all | solution.py:96
  205.7 2.6 mul.53
  208.3 4.9 %mul.54 = f32[16,32,2048]{2,1,0:T(8,128)} reshape(f32[16,32,16,128]{3,2,1,0:T(8,128)} %mul.53) | data formatting | bytes 8388608 | tf_op jit(solution)/shard_map/mul | solution.py:105
  213.2 60.7 %all-to-all-done.1 = bf16[16,32,2048]{2,1,0:T(8,128)(2,1)S(1)} async-done(((bf16[16,32,2048]{2,1,0:T(8,128)(2,1)}), bf16[16,32,2048]{2,1,0:T(8,128)(2,1)S(1)}, u32[]{:S(2)}, u32[]{:S(2)}) %all-to-all-start.1) | async-done | bytes 2097184 | tf_op jit(solution)/shard_map/all_to_all | solution.py:96
  273.9 2.8 %multiply_reduce_fusion = f32[32,2048]{1,0:T(8,128)S(1)} fusion(f32[16,32,2048]{2,1,0:T(8,128)} %mul.54, bf16[16,32,2048]{2,1,0:T(8,128)(2,1)S(1)} %all-to-all-done.1), kind=kLoop, calls=%fused_computation.40 | loop fusion | flops 3080192 | bytes 6553600 | tf_op jit(solution)/shard_map/reduce_sum | solution.py:105
  276.9 0.8 fusion.35
  (307 shorter events, 56.8 us)
Async XLA Ops:
  5.5 2.2 copy-start.2
  8.2 1.0 copy-start
  8.2 0.9 copy-start.1
  8.2 0.9 copy-start.3
  9.2 14.9 %collective-permute-start = (bf16[32,2048]{1,0:T(8,128)(2,1)S(1)}, bf16[32,2048]{1,0:T(8,128)(2,1)S(1)}, u32[]{:S(2)}, u32[]{:S(2)}) collective-permute-start(bf16[32,2048]{1,0:T(8,128)(2,1)S(1)} %get-tuple-element.402), channel_id=1, source_target_pairs={{0,32},{32,64},{64,96},{96,128},{128,160},{160,192},{192,224},{224... | collective-permute-start | bytes 393224 | tf_op jit(solution)/shard_map/while/body/eval_jaxpr/ppermute | solution.py:14
  26.0 8.1 %collective-permute-start = (bf16[32,2048]{1,0:T(8,128)(2,1)S(1)}, bf16[32,2048]{1,0:T(8,128)(2,1)S(1)}, u32[]{:S(2)}, u32[]{:S(2)}) collective-permute-start(bf16[32,2048]{1,0:T(8,128)(2,1)S(1)} %get-tuple-element.402), channel_id=1, source_target_pairs={{0,32},{32,64},{64,96},{96,128},{128,160},{160,192},{192,224},{224... | collective-permute-start | bytes 393224 | tf_op jit(solution)/shard_map/while/body/eval_jaxpr/ppermute | solution.py:14
  36.0 8.1 %collective-permute-start = (bf16[32,2048]{1,0:T(8,128)(2,1)S(1)}, bf16[32,2048]{1,0:T(8,128)(2,1)S(1)}, u32[]{:S(2)}, u32[]{:S(2)}) collective-permute-start(bf16[32,2048]{1,0:T(8,128)(2,1)S(1)} %get-tuple-element.402), channel_id=1, source_target_pairs={{0,32},{32,64},{64,96},{96,128},{128,160},{160,192},{192,224},{224... | collective-permute-start | bytes 393224 | tf_op jit(solution)/shard_map/while/body/eval_jaxpr/ppermute | solution.py:14
  46.0 8.1 %collective-permute-start = (bf16[32,2048]{1,0:T(8,128)(2,1)S(1)}, bf16[32,2048]{1,0:T(8,128)(2,1)S(1)}, u32[]{:S(2)}, u32[]{:S(2)}) collective-permute-start(bf16[32,2048]{1,0:T(8,128)(2,1)S(1)} %get-tuple-element.402), channel_id=1, source_target_pairs={{0,32},{32,64},{64,96},{96,128},{128,160},{160,192},{192,224},{224... | collective-permute-start | bytes 393224 | tf_op jit(solution)/shard_map/while/body/eval_jaxpr/ppermute | solution.py:14
  56.0 8.1 %collective-permute-start = (bf16[32,2048]{1,0:T(8,128)(2,1)S(1)}, bf16[32,2048]{1,0:T(8,128)(2,1)S(1)}, u32[]{:S(2)}, u32[]{:S(2)}) collective-permute-start(bf16[32,2048]{1,0:T(8,128)(2,1)S(1)} %get-tuple-element.402), channel_id=1, source_target_pairs={{0,32},{32,64},{64,96},{96,128},{128,160},{160,192},{192,224},{224... | collective-permute-start | bytes 393224 | tf_op jit(solution)/shard_map/while/body/eval_jaxpr/ppermute | solution.py:14
  66.0 8.1 %collective-permute-start = (bf16[32,2048]{1,0:T(8,128)(2,1)S(1)}, bf16[32,2048]{1,0:T(8,128)(2,1)S(1)}, u32[]{:S(2)}, u32[]{:S(2)}) collective-permute-start(bf16[32,2048]{1,0:T(8,128)(2,1)S(1)} %get-tuple-element.402), channel_id=1, source_target_pairs={{0,32},{32,64},{64,96},{96,128},{128,160},{160,192},{192,224},{224... | collective-permute-start | bytes 393224 | tf_op jit(solution)/shard_map/while/body/eval_jaxpr/ppermute | solution.py:14
  76.0 8.1 %collective-permute-start = (bf16[32,2048]{1,0:T(8,128)(2,1)S(1)}, bf16[32,2048]{1,0:T(8,128)(2,1)S(1)}, u32[]{:S(2)}, u32[]{:S(2)}) collective-permute-start(bf16[32,2048]{1,0:T(8,128)(2,1)S(1)} %get-tuple-element.402), channel_id=1, source_target_pairs={{0,32},{32,64},{64,96},{96,128},{128,160},{160,192},{192,224},{224... | collective-permute-start | bytes 393224 | tf_op jit(solution)/shard_map/while/body/eval_jaxpr/ppermute | solution.py:14
  85.9 9.2 %collective-permute-start = (bf16[32,2048]{1,0:T(8,128)(2,1)S(1)}, bf16[32,2048]{1,0:T(8,128)(2,1)S(1)}, u32[]{:S(2)}, u32[]{:S(2)}) collective-permute-start(bf16[32,2048]{1,0:T(8,128)(2,1)S(1)} %get-tuple-element.402), channel_id=1, source_target_pairs={{0,32},{32,64},{64,96},{96,128},{128,160},{160,192},{192,224},{224... | collective-permute-start | bytes 393224 | tf_op jit(solution)/shard_map/while/body/eval_jaxpr/ppermute | solution.py:14
  97.1 8.6 %collective-permute-start = (bf16[32,2048]{1,0:T(8,128)(2,1)S(1)}, bf16[32,2048]{1,0:T(8,128)(2,1)S(1)}, u32[]{:S(2)}, u32[]{:S(2)}) collective-permute-start(bf16[32,2048]{1,0:T(8,128)(2,1)S(1)} %get-tuple-element.402), channel_id=1, source_target_pairs={{0,32},{32,64},{64,96},{96,128},{128,160},{160,192},{192,224},{224... | collective-permute-start | bytes 393224 | tf_op jit(solution)/shard_map/while/body/eval_jaxpr/ppermute | solution.py:14
  107.6 8.1 %collective-permute-start = (bf16[32,2048]{1,0:T(8,128)(2,1)S(1)}, bf16[32,2048]{1,0:T(8,128)(2,1)S(1)}, u32[]{:S(2)}, u32[]{:S(2)}) collective-permute-start(bf16[32,2048]{1,0:T(8,128)(2,1)S(1)} %get-tuple-element.402), channel_id=1, source_target_pairs={{0,32},{32,64},{64,96},{96,128},{128,160},{160,192},{192,224},{224... | collective-permute-start | bytes 393224 | tf_op jit(solution)/shard_map/while/body/eval_jaxpr/ppermute | solution.py:14
  117.6 8.1 %collective-permute-start = (bf16[32,2048]{1,0:T(8,128)(2,1)S(1)}, bf16[32,2048]{1,0:T(8,128)(2,1)S(1)}, u32[]{:S(2)}, u32[]{:S(2)}) collective-permute-start(bf16[32,2048]{1,0:T(8,128)(2,1)S(1)} %get-tuple-element.402), channel_id=1, source_target_pairs={{0,32},{32,64},{64,96},{96,128},{128,160},{160,192},{192,224},{224... | collective-permute-start | bytes 393224 | tf_op jit(solution)/shard_map/while/body/eval_jaxpr/ppermute | solution.py:14
  127.6 8.1 %collective-permute-start = (bf16[32,2048]{1,0:T(8,128)(2,1)S(1)}, bf16[32,2048]{1,0:T(8,128)(2,1)S(1)}, u32[]{:S(2)}, u32[]{:S(2)}) collective-permute-start(bf16[32,2048]{1,0:T(8,128)(2,1)S(1)} %get-tuple-element.402), channel_id=1, source_target_pairs={{0,32},{32,64},{64,96},{96,128},{128,160},{160,192},{192,224},{224... | collective-permute-start | bytes 393224 | tf_op jit(solution)/shard_map/while/body/eval_jaxpr/ppermute | solution.py:14
  137.6 8.1 %collective-permute-start = (bf16[32,2048]{1,0:T(8,128)(2,1)S(1)}, bf16[32,2048]{1,0:T(8,128)(2,1)S(1)}, u32[]{:S(2)}, u32[]{:S(2)}) collective-permute-start(bf16[32,2048]{1,0:T(8,128)(2,1)S(1)} %get-tuple-element.402), channel_id=1, source_target_pairs={{0,32},{32,64},{64,96},{96,128},{128,160},{160,192},{192,224},{224... | collective-permute-start | bytes 393224 | tf_op jit(solution)/shard_map/while/body/eval_jaxpr/ppermute | solution.py:14
  147.6 8.1 %collective-permute-start = (bf16[32,2048]{1,0:T(8,128)(2,1)S(1)}, bf16[32,2048]{1,0:T(8,128)(2,1)S(1)}, u32[]{:S(2)}, u32[]{:S(2)}) collective-permute-start(bf16[32,2048]{1,0:T(8,128)(2,1)S(1)} %get-tuple-element.402), channel_id=1, source_target_pairs={{0,32},{32,64},{64,96},{96,128},{128,160},{160,192},{192,224},{224... | collective-permute-start | bytes 393224 | tf_op jit(solution)/shard_map/while/body/eval_jaxpr/ppermute | solution.py:14
  157.6 8.2 %collective-permute-start = (bf16[32,2048]{1,0:T(8,128)(2,1)S(1)}, bf16[32,2048]{1,0:T(8,128)(2,1)S(1)}, u32[]{:S(2)}, u32[]{:S(2)}) collective-permute-start(bf16[32,2048]{1,0:T(8,128)(2,1)S(1)} %get-tuple-element.402), channel_id=1, source_target_pairs={{0,32},{32,64},{64,96},{96,128},{128,160},{160,192},{192,224},{224... | collective-permute-start | bytes 393224 | tf_op jit(solution)/shard_map/while/body/eval_jaxpr/ppermute | solution.py:14
  169.2 25.5 %all-to-all-start = ((f32[16,1,512]{2,1,0:T(1,128)}), f32[16,1,512]{2,1,0:T(1,128)S(1)}, u32[]{:S(2)}, u32[]{:S(2)}) async-start(f32[16,1,512]{2,1,0:T(1,128)} %reshape.345), calls=%async_computation | async-start | bytes 65536 | tf_op jit(solution)/shard_map/all_to_all | solution.py:99
  194.7 79.2 %all-to-all-start.1 = ((bf16[16,32,2048]{2,1,0:T(8,128)(2,1)}), bf16[16,32,2048]{2,1,0:T(8,128)(2,1)S(1)}, u32[]{:S(2)}, u32[]{:S(2)}) async-start(bf16[16,32,2048]{2,1,0:T(8,128)(2,1)} %select_convert_fusion), calls=%async_computation.1 | async-start | bytes 4194304 | tf_op jit(solution)/shard_map/all_to_all | solution.py:96
where the time goes:
time: 279 us; the launch traced here: 278 us
  waiting for transfers between devices  146 us (52%)
  starting transfers between devices  49.8 us (18%)
  other arithmetic  46 us (16%)
  matrix products  18.3 us (7%)
  local copies, waits for them, and re-layouts  15.7 us (6%)
    ppermute x15, waiting for transfers between devices, passed_along(): lax.ppermute(x, axis, [(i, (i + by) % length) for i in range(length)])  74.2 us
    all_to_all x1, waiting for transfers between devices, per_device(): lax.all_to_all(routed[0].astype(jnp.float32), 'ctx', split_axis=0, concat...  60.7 us
    ppermute x15, starting transfers between devices, passed_along(): lax.ppermute(x, axis, [(i, (i + by) % length) for i in range(length)])  30.7 us
    reduce_sum x32, other arithmetic, select_entry(): return jnp.sum(jnp.where(hits, table, 0), axis=table.ndim - 1)  13.2 us
    all_to_all x1, waiting for transfers between devices, per_device(): lax.all_to_all(routed[1], 'ctx', split_axis=0, concat_axis=0, tiled=True)  10.6 us
    reduce_sum x16, other arithmetic, shard_partial(): total = jnp.maximum(jnp.sum(weights, axis=3), 1.0)  9.92 us
    dot_general x16, matrix products, shard_partial(): jnp.einsum('qgjd,kgd->gjqk', query, key_tiles, preferred_element_type=jnp...  9.67 us
    all_to_all x1, starting transfers between devices, per_device(): lax.all_to_all(routed[1], 'ctx', split_axis=0, concat_axis=0, tiled=True)  9.61 us
  transfers between devices with their start and end apart: 17, of which 17 were waited for; matrix products, arithmetic and copies ran while one was open for 14% of the time, Pallas kernels for 0%

commit v1 on v0

v1 whole, which is shorter than its diff:
```python
import math

import jax
import jax.numpy as jnp
from jax import lax
from jax.experimental import pallas as pl
from jax.experimental.pallas import tpu as pltpu
from jax.sharding import PartitionSpec as P

HD = 128
NEG = -1e30
MESH = pl.DeviceIdType.MESH
CHUNKS = 4
RIGHT, LEFT = 0, 1


def kernel(
    queries, cached_keys, cached_values, turn_lengths, tile_map, prefix_len, owner_ids,
    result,
    blocks, partials, spreads, keys, values, key_cols, value_cols, inverse, merged,
    arrived, leaving, arrived_spread, leaving_spread,
    load_sem, gather_send, gather_recv, part_send, part_recv, spread_send, spread_recv, store_sem,
):
    n = blocks.shape[0]
    rows = blocks.shape[2]
    width = blocks.shape[3]
    per_chunk = width // HD
    groups = rows // 8
    heads = CHUNKS * per_chunk
    cache = keys.shape[0]
    turns = turn_lengths.shape[0]
    reach = n // 2
    half = CHUNKS // 2
    me = lax.axis_index("ctx")
    right, left = lax.rem(me + 1, n), lax.rem(me + n - 1, n)
    to = ({"ctx": right}, {"ctx": left})
    scale2 = HD ** (-0.5) * math.log2(math.e)

    def place(offset):
        return lax.rem(me + offset + n, n)

    def chunk_of(side, position):
        return position if side == RIGHT else CHUNKS - 1 - position

    key_load = pltpu.make_async_copy(cached_keys, keys, load_sem.at[CHUNKS])
    value_load = pltpu.make_async_copy(cached_values, values, load_sem.at[CHUNKS + 1])
    own_loads = [
        pltpu.make_async_copy(
            queries.at[:, pl.ds(c * width, width)], blocks.at[me, c], load_sem.at[c]
        )
        for c in range(CHUNKS)
    ]
    for load in own_loads:
        load.start()
    key_load.start()
    value_load.start()

    barrier = pltpu.get_barrier_semaphore()
    for side in (RIGHT, LEFT):
        pl.semaphore_signal(barrier, inc=1, device_id=to[side], device_id_type=MESH)
    pl.semaphore_wait(barrier, 2)

    def gather_copy(side, step, block, c):
        return pltpu.make_async_remote_copy(
            src_ref=blocks.at[block, c],
            dst_ref=blocks.at[block, c],
            send_sem=gather_send.at[side, step, c],
            recv_sem=gather_recv.at[side, step, c],
            device_id=to[side],
            device_id_type=MESH,
        )

    def part_copy(side, step, c):
        return pltpu.make_async_remote_copy(
            src_ref=leaving.at[side, step, c],
            dst_ref=arrived.at[side, step, c],
            send_sem=part_send.at[side, step, c],
            recv_sem=part_recv.at[side, step, c],
            device_id=to[side],
            device_id_type=MESH,
        )

    def spread_copy(side, step):
        return pltpu.make_async_remote_copy(
            src_ref=leaving_spread.at[side, step],
            dst_ref=arrived_spread.at[side, step],
            send_sem=spread_send.at[side, step],
            recv_sem=spread_recv.at[side, step],
            device_id=to[side],
            device_id_type=MESH,
        )

    for load in own_loads:
        load.wait()
    for position in range(CHUNKS):
        for side in (RIGHT, LEFT):
            gather_copy(side, 0, me, chunk_of(side, position)).start()

    for owner in range(n):
        source = jnp.int32(0)
        for b in range(n):
            source = jnp.maximum(source, jnp.where(owner_ids[b] == owner, b, 0))
        inverse[owner] = source
    limit = prefix_len[me]
    bounds = []
    begin = jnp.int32(0)
    for t in range(turns):
        end = begin + turn_lengths[t]
        bounds.append((begin, end, tile_map[t, me]))
        begin = end

    key_load.wait()
    value_load.wait()
    live = lax.broadcasted_iota(jnp.int32, (cache, HD), 0) < limit
    key_all = keys[...].astype(jnp.float32)
    key_all = jnp.where(live, key_all, jnp.broadcast_to(key_all[0:1, :], (cache, HD)))
    key_cols[...] = key_all.T.astype(jnp.bfloat16)
    value_cols[:, 0:HD] = jnp.where(live, values[...].astype(jnp.float32), 0.0).astype(jnp.bfloat16)
    value_cols[:, HD:2 * HD] = jnp.where(live, 1.0, 0.0).astype(jnp.bfloat16)

    lane = lax.broadcasted_iota(jnp.int32, (8, HD), 1)
    sublane = lax.broadcasted_iota(jnp.int32, (8, HD), 0)

    def compute(pairs):
        query = jnp.concatenate(
            [
                blocks[block, c, :, pl.ds(j * HD, HD)]
                for block, c in pairs
                for j in range(per_chunk)
            ],
            axis=0,
        )
        scores = jnp.dot(query, key_cols[...], preferred_element_type=jnp.float32)
        peak = jnp.max(scores, axis=1, keepdims=True)
        weights = jnp.exp2((scores - peak) * scale2).astype(jnp.bfloat16)
        mixed = jnp.dot(weights, value_cols[...], preferred_element_type=jnp.float32)
        total = jnp.maximum(mixed[:, HD:2 * HD], 1.0)
        part = (mixed[:, 0:HD] / total).astype(jnp.bfloat16)
        spread = peak * scale2 + jnp.log2(total)
        at = 0
        for block, c in pairs:
            packed = jnp.zeros((8, HD), jnp.float32)
            for j in range(per_chunk):
                partials[block, c, :, pl.ds(j * HD, HD)] = part[at:at + rows]
                for i in range(groups):
                    slot = i * heads + c * per_chunk + j
                    packed = jnp.where(lane == slot, spread[at + 8 * i:at + 8 * i + 8], packed)
                at += rows
            spreads[block, c] = packed

    for c in range(0, CHUNKS, 2):
        compute([(me, c), (me, c + 1)])

    def gather_step(step, carry):
        b_right, b_left = place(-step), place(step)
        for position in range(CHUNKS):
            c_right, c_left = chunk_of(RIGHT, position), chunk_of(LEFT, position)
            for side, block, c in ((RIGHT, b_right, c_right), (LEFT, b_left, c_left)):
                gather_copy(side, step - 1, block, c).wait_recv()
                if position < half:
                    gather_copy(side, step, block, c).start()
                else:
                    @pl.when(step < reach - 1)
                    def _():
                        gather_copy(side, step, block, c).start()
            compute([(b_right, c_right), (b_left, c_left)])
            for side, block, c in ((RIGHT, b_right, c_right), (LEFT, b_left, c_left)):
                gather_copy(side, step - 1, block, c).wait_send()
        return carry

    lax.fori_loop(1, reach, gather_step, 0)
    far = place(reach)
    for position in range(half):
        pairs = [(far, chunk_of(side, position)) for side in (RIGHT, LEFT)]
        for side in (RIGHT, LEFT):
            gather_copy(side, reach - 1, far, pairs[side][1]).wait_recv()
        compute(pairs)

    def own_spread(block):
        spread = spreads[block, 0]
        for c in range(1, CHUNKS):
            spread = spread + spreads[block, c]
        row = block * rows + 8 * (lane // heads) + sublane
        sees = jnp.zeros((8, HD), jnp.int32)
        for begin, end, seen in bounds:
            sees = sees + jnp.where((row >= begin) & (row < end), seen, 0)
        return jnp.where((sees > 0) & (lane < groups * heads), spread, NEG)

    def along_rows(packed, c, j):
        slots = [i * heads + c * per_chunk + j for i in range(groups)]
        return jnp.concatenate(
            [jnp.broadcast_to(packed[:, s:s + 1], (8, HD)) for s in slots], axis=0
        )

    def pick(block, c, j):
        return partials[block, c, :, pl.ds(j * HD, HD)].astype(jnp.float32)

    def owner_at(side, step):
        return place(reach - step) if side == RIGHT else place(step - reach)

    far = inverse[place(reach)]
    for side in (RIGHT, LEFT):
        mine = (lane % heads) // per_chunk
        mine = mine < half if side == RIGHT else mine >= half
        leaving_spread[side, 0] = jnp.where(mine, own_spread(far), NEG)
        spread_copy(side, 0).start()
    for position in range(half):
        for side in (RIGHT, LEFT):
            c = chunk_of(side, position)
            leaving[side, 0, c] = partials[far, c]
            part_copy(side, 0, c).start()

    def merge_step(step, first):
        sources, keeps = [], []
        for side in (RIGHT, LEFT):
            source = inverse[owner_at(side, step)]
            spread_copy(side, step - 1).wait_recv()
            so_far, here = arrived_spread[side, step - 1], own_spread(source)
            top = jnp.maximum(so_far, here)
            both = top + jnp.log2(jnp.exp2(so_far - top) + jnp.exp2(here - top))
            leaving_spread[side, step] = both
            spread_copy(side, step).start()
            sources.append(source)
            keeps.append(jnp.exp2(so_far - both))
        for position in range(CHUNKS):
            for side in (RIGHT, LEFT):
                c = chunk_of(side, position)
                if first and position >= half:
                    leaving[side, step, c] = partials[sources[side], c]
                else:
                    part_copy(side, step - 1, c).wait_recv()
                    for j in range(per_chunk):
                        keep = along_rows(keeps[side], c, j)
                        before = arrived[side, step - 1, c, :, pl.ds(j * HD, HD)].astype(jnp.float32)
                        now = before * keep + pick(sources[side], c, j) * (1.0 - keep)
                        leaving[side, step, c, :, pl.ds(j * HD, HD)] = now.astype(jnp.bfloat16)
                part_copy(side, step, c).start()
        for side in (RIGHT, LEFT):
            spread_copy(side, step - 1).wait_send()
            for position in range(half if first else CHUNKS):
                part_copy(side, step - 1, chunk_of(side, position)).wait_send()

    merge_step(1, True)

    def merge_loop(step, carry):
        merge_step(step, False)
        return carry

    lax.fori_loop(2, reach, merge_loop, 0)

    source = inverse[me]
    for side in (RIGHT, LEFT):
        spread_copy(side, reach - 1).wait_recv()
    terms = [arrived_spread[RIGHT, reach - 1], arrived_spread[LEFT, reach - 1], own_spread(source)]
    top = jnp.maximum(jnp.maximum(terms[0], terms[1]), terms[2])
    terms = [jnp.exp2(term - top) for term in terms]
    total = terms[0] + terms[1] + terms[2]
    terms = [term / total for term in terms]
    stores = []
    for position in range(CHUNKS):
        c = position // 2 if position % 2 == 0 else CHUNKS - 1 - position // 2
        for side in (RIGHT, LEFT):
            part_copy(side, reach - 1, c).wait_recv()
        for j in range(per_chunk):
            full = pick(source, c, j) * along_rows(terms[2], c, j)
            for side in (RIGHT, LEFT):
                come = arrived[side, reach - 1, c, :, pl.ds(j * HD, HD)].astype(jnp.float32)
                full = full + come * along_rows(terms[side], c, j)
            merged[:, pl.ds(c * width + j * HD, HD)] = full.astype(jnp.bfloat16)
        columns = pl.ds(c * width, width)
        store = pltpu.make_async_copy(merged.at[:, columns], result.at[:, columns], store_sem.at[c])
        store.start()
        stores.append(store)
    for side in (RIGHT, LEFT):
        for position in range(half):
            gather_copy(side, reach - 1, me, chunk_of(side, position)).wait_send()
        spread_copy(side, reach - 1).wait_send()
        for c in range(CHUNKS):
            part_copy(side, reach - 1, c).wait_send()
    for store in stores:
        store.wait()


def per_device(queries, cached_keys, cached_values, turn_lengths, tile_map, prefix_len, owner_ids):
    n = lax.axis_size("ctx")
    rows, columns = queries.shape
    cache = cached_keys.shape[0]
    width = columns // CHUNKS
    reach = n // 2
    hbm = pl.BlockSpec(memory_space=pl.ANY)
    smem = pl.BlockSpec(memory_space=pltpu.SMEM)
    dma = pltpu.SemaphoreType.DMA
    return pl.pallas_call(
        kernel,
        out_shape=jax.ShapeDtypeStruct((rows, columns), jnp.bfloat16),
        in_specs=[hbm] * 3 + [smem] * 4,
        out_specs=hbm,
        scratch_shapes=[
            pltpu.VMEM((n, CHUNKS, rows, width), jnp.bfloat16),
            pltpu.VMEM((n, CHUNKS, rows, width), jnp.bfloat16),
            pltpu.VMEM((n, CHUNKS, 8, HD), jnp.float32),
            pltpu.VMEM((cache, HD), jnp.bfloat16),
            pltpu.VMEM((cache, HD), jnp.bfloat16),
            pltpu.VMEM((HD, cache), jnp.bfloat16),
            pltpu.VMEM((cache, 2 * HD), jnp.bfloat16),
            pltpu.SMEM((n,), jnp.int32),
            pltpu.VMEM((rows, columns), jnp.bfloat16),
            pltpu.VMEM((2, reach, CHUNKS, rows, width), jnp.bfloat16),
            pltpu.VMEM((2, reach, CHUNKS, rows, width), jnp.bfloat16),
            pltpu.VMEM((2, reach, 8, HD), jnp.float32),
            pltpu.VMEM((2, reach, 8, HD), jnp.float32),
            dma((CHUNKS + 2,)),
            dma((2, reach, CHUNKS)),
            dma((2, reach, CHUNKS)),
            dma((2, reach, CHUNKS)),
            dma((2, reach, CHUNKS)),
            dma((2, reach)),
            dma((2, reach)),
            dma((CHUNKS,)),
        ],
        compiler_params=pltpu.CompilerParams(
            collective_id=0, has_side_effects=True, vmem_limit_bytes=48 * 1024 * 1024
        ),
        cost_estimate=pl.CostEstimate(
            flops=4 * n * rows * columns * cache, bytes_accessed=1 << 20, transcendentals=n * rows * columns * cache // HD
        ),
    )(queries, cached_keys, cached_values, turn_lengths, tile_map, prefix_len, owner_ids)


def solution(mesh):
    return jax.shard_map(
        per_device,
        mesh=mesh,
        in_specs=(
            P(("pack", "ctx"), "head"),
            P(("pack", "ctx"), "head"),
            P(("pack", "ctx"), "head"),
            P("pack"),
            P("pack", None),
            P("pack"),
            P("pack"),
        ),
        out_specs=P(("pack", "ctx"), "head"),
        check_vma=False,
    )
```

time: 279 us -> 81 us (0.29)
  waiting for transfers between devices: 146 us -> 0 us
  Pallas kernels: 0 us -> 74.1 us
  starting transfers between devices: 49.8 us -> 0 us
  other arithmetic: 46 us -> 0 us
  matrix products: 18.3 us -> 0 us
  local copies, waits for them, and re-layouts: 15.7 us -> 6.11 us
    ppermute x15 -> x0, waiting for transfers between devices: 74.2 us -> none  [passed_along(): lax.ppermute(x, axis, [(i, (i + by) % length) for i in range(length)])]
    pallas_call x0 -> x1, Pallas kernels: none -> 74.1 us  [per_device(): pl.pallas_call(kernel, out_shape=jax.ShapeDtypeStruct((rows, columns), jn...]
    all_to_all x2 -> x0, waiting for transfers between devices: 71.3 us -> none  [the longest x1 60.7 us: per_device(): lax.all_to_all(routed[0].astype(jnp.float32), 'ctx', split_axis=0, concat...]
    ppermute x15 -> x0, starting transfers between devices: 30.7 us -> none  [passed_along(): lax.ppermute(x, axis, [(i, (i + by) % length) for i in range(length)])]
    reduce_sum x83 -> x0, other arithmetic: 29.5 us -> none  [the longest x32 13.2 us: select_entry(): return jnp.sum(jnp.where(hits, table, 0), axis=table.ndim - 1)]
    all_to_all x2 -> x0, starting transfers between devices: 19.1 us -> none  [the longest x1 9.61 us: per_device(): lax.all_to_all(routed[1], 'ctx', split_axis=0, concat_axis=0, tiled=True)]
    dot_general x32 -> x0, matrix products: 18.3 us -> none  [the longest x16 9.67 us: shard_partial(): jnp.einsum('qgjd,kgd->gjqk', query, key_tiles, preferred_element_type=jnp...]
    lt x16 -> x0, other arithmetic: 8.99 us -> none  [tile_partial(): key_live = lax.iota(jnp.int32, shard_rows) < limit]
  transfers between devices with their start and end apart: 17 -> 0, of which waited for: 17 -> 0; matrix products, arithmetic and copies ran while one was open for 14% -> 0% of each run, Pallas kernels for 0% -> 0%
where the time goes in v1:
time: 81 us; the launch traced here: 80.3 us
  Pallas kernels  74.1 us (91%)
  local copies, waits for them, and re-layouts  6.11 us (8%)
    pallas_call x1, Pallas kernels, per_device(): pl.pallas_call(kernel, out_shape=jax.ShapeDtypeStruct((rows, columns), jn...  74.1 us
    unnamed x15, local copies, waits for them, and re-layouts  6.11 us

profile of v1, /device:TPU:24, one launch (start us, length us, event | category | flops | bytes accessed | tf_op | source)
XLA Modules:
  0.0 80.3 jit_solution(2024792222870697623)
XLA Ops:
  0.0 0.0 copy-start
  0.0 0.9 %copy-done = bf16[1024,128]{1,0:T(8,128)(2,1)S(1)} copy-done((bf16[1024,128]{1,0:T(8,128)(2,1)S(1)}, bf16[1024,128]{1,0:T(8,128)(2,1)}, u32[]{:S(2)}) %copy-start) | copy-done | bytes 262168
  1.0 0.0 copy-start.1
  1.0 0.9 %copy-done.1 = bf16[1024,128]{1,0:T(8,128)(2,1)S(1)} copy-done((bf16[1024,128]{1,0:T(8,128)(2,1)S(1)}, bf16[1024,128]{1,0:T(8,128)(2,1)}, u32[]{:S(2)}) %copy-start.1) | copy-done | bytes 262168
  1.9 0.0 copy-start.2
  1.9 0.9 %copy-done.2 = bf16[32,2048]{1,0:T(8,128)(2,1)S(1)} copy-done((bf16[32,2048]{1,0:T(8,128)(2,1)S(1)}, bf16[32,2048]{1,0:T(8,128)(2,1)}, u32[]{:S(2)}) %copy-start.2) | copy-done | bytes 131096
  2.8 0.0 copy-start.3
  2.8 0.7 copy-done.3
  3.5 0.0 copy-start.4
  3.5 0.7 copy-done.4
  4.1 0.0 copy-start.5
  4.2 0.7 copy-done.5
  4.8 0.0 copy-start.6
  4.8 0.7 copy-done.6
  5.5 74.1 %shard_map.73 = bf16[32,2048]{1,0:T(8,128)(2,1)S(1)} custom-call(bf16[32,2048]{1,0:T(8,128)(2,1)S(1)} %copy-done.2, bf16[1024,128]{1,0:T(8,128)(2,1)S(1)} %copy-done, bf16[1024,128]{1,0:T(8,128)(2,1)S(1)} %copy-done.1, s32[8]{0:T(128)S(1)} %copy-done.4, s32[8,16]{1,0:T(8,128)S(1)} %copy-done.3, s32[16]{0:T(128)S(1)} %copy-done.5, s32[16]{0:T(128)S(1)} %copy-done.6), custom_call_target="tpu_custom_call" | custom-call | flops 4294967296 | bytes 1048576 | tf_op jit(solution)/shard_map/pallas_call | solution.py:293
  79.6 0.7 copy.9
Async XLA Ops:
  0.0 0.9 %copy-start = (bf16[1024,128]{1,0:T(8,128)(2,1)S(1)}, bf16[1024,128]{1,0:T(8,128)(2,1)}, u32[]{:S(2)}) copy-start(bf16[1024,128]{1,0:T(8,128)(2,1)} %cached_keys.1) | copy-start | bytes 786436
  1.0 0.9 %copy-start.1 = (bf16[1024,128]{1,0:T(8,128)(2,1)S(1)}, bf16[1024,128]{1,0:T(8,128)(2,1)}, u32[]{:S(2)}) copy-start(bf16[1024,128]{1,0:T(8,128)(2,1)} %cached_values.1) | copy-start | bytes 786436
  1.9 0.9 %copy-start.2 = (bf16[32,2048]{1,0:T(8,128)(2,1)S(1)}, bf16[32,2048]{1,0:T(8,128)(2,1)}, u32[]{:S(2)}) copy-start(bf16[32,2048]{1,0:T(8,128)(2,1)} %queries.1) | copy-start | bytes 393220
  2.8 0.7 copy-start.3
  3.5 0.7 copy-start.4
  4.1 0.7 copy-start.5
  4.8 0.7 copy-start.6

commit v2 on v0

v2 whole, which is shorter than its diff:
```python
import math

import jax
import jax.numpy as jnp
from jax import lax
from jax.experimental import pallas as pl
from jax.experimental.pallas import tpu as pltpu
from jax.sharding import PartitionSpec as P

HD = 128
NEG = -1e30
MESH = pl.DeviceIdType.MESH
CHUNKS = 4
HALF = CHUNKS // 2
RIGHT, LEFT = 0, 1
SIDES = (RIGHT, LEFT)
KV_PIECES = 4
COUNT_ROWS = 16


def kernel(
    queries, cached_keys, cached_values, turn_lengths_in, tile_map_in, prefix_len_in, owner_ids_in,
    result,
    turn_lengths, tile_map, prefix_len, owner_ids, inverse,
    others, blocks, partials, spreads, keys, values, key_rows, value_cols, merged,
    arrived, leaving, arrived_spread, leaving_spread,
    load_sem, table_sem, kv_load, kv_send, kv_recv, gather_send, gather_recv,
    part_send, part_recv, spread_send, spread_recv, store_sem,
):
    n, _, rows, width = blocks.shape
    per_chunk = width // HD
    lanes = per_chunk * rows
    cache = keys.shape[1]
    piece = cache // KV_PIECES
    turns = turn_lengths.shape[0]
    steps = n // 4
    scale2 = HD ** (-0.5) * math.log2(math.e)
    me = lax.axis_index("ctx")
    core = lax.rem(lax.axis_index("pack"), 2)
    parity = lax.rem(me + core, 2)

    def place(offset):
        return lax.rem(me + offset + n, n)

    partner = place(1 - 2 * parity)

    def device(index):
        return {"ctx": index}

    def ahead(side, by):
        return place(by) if side == RIGHT else place(-by)

    def columns(c):
        return pl.ds(pl.multiple_of(c * width, width), width)

    own_loads = [
        pltpu.make_async_copy(
            queries.at[:, columns(HALF * parity + u)], blocks.at[me, u], load_sem.at[u]
        )
        for u in range(HALF)
    ]
    other_loads = [
        pltpu.make_async_copy(
            queries.at[:, columns(HALF * (1 - parity) + u)], others.at[u], load_sem.at[HALF + u]
        )
        for u in range(HALF)
    ]
    kv_loads = [
        pltpu.make_async_copy(cached_keys, keys.at[0], kv_load.at[0]),
        pltpu.make_async_copy(cached_values, values.at[0], kv_load.at[1]),
    ]
    tables = [
        pltpu.make_async_copy(source, target, table_sem.at[i])
        for i, (source, target) in enumerate(
            (
                (turn_lengths_in, turn_lengths),
                (tile_map_in, tile_map),
                (prefix_len_in, prefix_len),
                (owner_ids_in, owner_ids),
            )
        )
    ]
    for load in own_loads + other_loads + kv_loads + tables:
        load.start()

    barrier = pltpu.get_barrier_semaphore()
    for side in SIDES:
        for by in (1, 2):
            pl.semaphore_signal(
                barrier, inc=1, device_id=device(ahead(side, by)), device_id_type=MESH
            )
    pl.semaphore_wait(barrier, 4)

    def remote(source, target, send_sem, recv_sem, index):
        return pltpu.make_async_remote_copy(
            src_ref=source, dst_ref=target, send_sem=send_sem, recv_sem=recv_sem,
            device_id=device(index), device_id_type=MESH,
        )

    def gather_copy(side, step, kind, u, block, own_other=False):
        return remote(
            others.at[u] if own_other else blocks.at[block, u],
            blocks.at[block, u],
            gather_send.at[side, step, kind, u],
            gather_recv.at[side, step, kind, u],
            ahead(side, 1 if own_other else 2),
        )

    def kv_copy(which, p):
        source, target = ((cached_keys, keys), (cached_values, values))[which]
        part = pl.ds(p * piece, piece)
        return remote(
            source.at[part], target.at[1, part], kv_send.at[which, p], kv_recv.at[which, p], partner
        )

    def order(position):
        return (position % 2, position // 2) if isinstance(position, int) else (lax.rem(position, 2), position // 2)

    def goes_on(side, kind, u, step, last):
        return (step < last) | ((step == last) & ((kind == 1) | (u == side)))

    for load in own_loads + other_loads:
        load.wait()
    for u in range(HALF):
        for kind in range(2):
            for side in SIDES:
                gather_copy(side, 0, kind, u, me, own_other=kind == 1).start()
        if u == HALF - 1:
            for which in range(2):
                for p in range(KV_PIECES):
                    kv_copy(which, p).start()

    for table in tables:
        table.wait()
    for owner in range(n):
        source = jnp.int32(0)
        for b in range(n):
            source = jnp.maximum(source, jnp.where(owner_ids[b] == owner, b, 0))
        inverse[owner] = source
    shards = (me, partner)
    bounds = []
    begin = jnp.int32(0)
    for t in range(turns):
        end = begin + turn_lengths[t]
        bounds.append((begin, end, tile_map[t, me], tile_map[t, partner]))
        begin = end

    def prepare(s):
        limit = prefix_len[shards[s]]
        live = lax.broadcasted_iota(jnp.int32, (cache, HD), 0) < limit
        key_all = keys[s].astype(jnp.float32) * scale2
        key_all = jnp.where(live, key_all, jnp.broadcast_to(key_all[0:1, :], (cache, HD)))
        high = key_all.astype(jnp.bfloat16)
        key_rows[s, :, 0:HD] = high
        key_rows[s, :, HD:2 * HD] = (key_all - high.astype(jnp.float32)).astype(jnp.bfloat16)
        value_all = jnp.where(live, values[s].astype(jnp.float32), 0.0)
        value_cols[s, 0:HD, :] = value_all.T.astype(jnp.bfloat16)
        counted = lax.broadcasted_iota(jnp.int32, (COUNT_ROWS, cache), 1) < limit
        value_cols[s, HD:HD + COUNT_ROWS, :] = jnp.where(counted, 1.0, 0.0).astype(jnp.bfloat16)

    lane = lax.broadcasted_iota(jnp.int32, (2, lanes), 1)
    even_row = lax.broadcasted_iota(jnp.int32, (2, lanes), 0) == 0


    def score(s, pairs):
        query = jnp.concatenate(
            [
                blocks[block, u, :, pl.ds(j * HD, HD)]
                for block, u in pairs
                for j in range(per_chunk)
            ],
            axis=0,
        )
        query = jnp.concatenate([query, query], axis=1)
        scores = lax.dot_general(
            key_rows[s], query, (((1,), (1,)), ((), ())), preferred_element_type=jnp.float32
        )
        peak = jnp.max(scores.reshape(cache // 32, 32, scores.shape[1]), axis=0)
        return scores, jnp.max(peak, axis=0, keepdims=True)

    def absorb(s, pairs, scores, peak):
        weights = jnp.exp2(scores - peak).astype(jnp.bfloat16)
        mixed = jnp.dot(value_cols[s], weights, preferred_element_type=jnp.float32)
        total = jnp.maximum(mixed[HD:HD + 1, :], 1.0)
        part = (mixed[0:HD, :] * (1.0 / total)).astype(jnp.bfloat16)
        spread = peak + jnp.log2(total)
        for i, (block, u) in enumerate(pairs):
            partials[s, block, u] = part[:, i * lanes:(i + 1) * lanes]
            spreads[s, block, u] = jnp.broadcast_to(
                spread[:, i * lanes:(i + 1) * lanes], (2, lanes)
            )

    def compute(*units):
        ahead_of = score(*units[0])
        for i, unit in enumerate(units):
            now = ahead_of
            if i + 1 < len(units):
                ahead_of = score(*units[i + 1])
            absorb(*unit, *now)

    def block_at(side, step, kind):
        return place(kind - 2 * step) if side == RIGHT else place(2 * step - kind)

    def pairs_at(step, position):
        kind, u = order(position)
        return [(block_at(side, step, kind), u) for side in SIDES]

    def arrive(step, position, sides=SIDES):
        kind, u = order(position)
        for side in sides:
            block = block_at(side, step, kind)
            gather_copy(side, step - 1, kind, u, block).wait_recv()
            if isinstance(step, int) and step == steps:
                continue

            @pl.when(goes_on(side, kind, u, step, steps - 1))
            def _():
                gather_copy(side, step, kind, u, block).start()

    def sent(step, position):
        kind, u = order(position)
        for side in SIDES:
            gather_copy(side, step, kind, u, me).wait_send()

    own_pairs = [(me, 0), (me, 1)]
    for load in kv_loads:
        load.wait()
    prepare(0)
    compute((0, own_pairs))

    def early_step(it, carry):
        step, position = it // CHUNKS, lax.rem(it, CHUNKS)
        arrive(step, position)
        compute((0, pairs_at(step, position)))
        return carry

    lax.fori_loop(CHUNKS, 3 * CHUNKS, early_step, 0)
    for which in range(2):
        for p in range(KV_PIECES):
            kv_copy(which, p).wait_recv()
    prepare(1)
    compute((1, own_pairs))

    def late_step(position, carry):
        arrive(3, position)
        compute(
            (0, pairs_at(3, position)), *[(1, pairs_at(step, position)) for step in range(1, 4)]
        )
        for step in range(1, 4):
            sent(step - 1, position)
        return carry

    lax.fori_loop(0, CHUNKS, late_step, 0)

    def last_step(u):
        units = []
        for kind in range(2):
            sides = SIDES if kind == 1 else (u,)
            arrive(steps, 2 * u + kind, sides)
            pairs = [(block_at(side, steps, kind), u) for side in sides]
            units = units + [(0, pairs), (1, pairs)]
        compute(*units)

    def own_spread(s, even, odd, u):
        spread = jnp.where(even_row, spreads[s, even, u], spreads[s, odd, u])
        row = jnp.where(even_row, even, odd) * rows + lax.rem(lane, rows)
        sees = jnp.zeros((2, lanes), jnp.int32)
        for bound in bounds:
            sees = sees + jnp.where((row >= bound[0]) & (row < bound[1]), bound[2 + s], 0)
        return jnp.where(sees > 0, spread, NEG)

    def part_copy(side, step, kind, u):
        return remote(
            leaving.at[side, step, kind, u],
            arrived.at[side, step, kind, u],
            part_send.at[side, step, kind, u],
            part_recv.at[side, step, kind, u],
            ahead(side, 1 if step == steps - 1 and kind == 1 else 2),
        )

    def spread_copy(side, step, u, kind=0):
        to = step + 1 if kind == 1 else step
        return remote(
            leaving_spread.at[side, step, u],
            arrived_spread.at[side, to, u],
            spread_send.at[side, to, u],
            spread_recv.at[side, to, u],
            ahead(side, 1 if kind == 1 else 2),
        )

    def weights_of(terms):
        top = terms[0]
        for term in terms[1:]:
            top = jnp.maximum(top, term)
        terms = [jnp.exp2(term - top) for term in terms]
        total = terms[0]
        for term in terms[1:]:
            total = total + term
        return [term / total for term in terms], top + jnp.log2(total)

    def mix(kind, sources):
        full = None
        for weight, term in sources:
            term = term.astype(jnp.float32) * weight[kind:kind + 1, :]
            full = term if full is None else full + term
        return full

    def starts(side, kind, u, step):
        return step == 0 or (step == 1 and kind == 0 and u != side)

    def merge_step(step, u):
        for side in SIDES:
            far = 2 * (steps - step)
            blocks_of = [inverse[ahead(side, far)], inverse[ahead(side, far - 1)]]
            terms = [own_spread(s, *blocks_of, u) for s in range(2)]
            if step == 0:
                if u != side:
                    terms = [jnp.where(even_row, NEG, term) for term in terms]
            else:
                spread_copy(side, step - 1, u).wait_recv()
                terms.append(arrived_spread[side, step - 1, u])
            weights, spread = weights_of(terms)
            leaving_spread[side, step, u] = spread
            spread_copy(side, step, u).start()
            if step == steps - 1:
                spread_copy(side, step, u, 1).start()
            for kind in range(2):
                if step == 0 and kind == 0 and u != side:
                    continue
                come = [(weights[s], partials[s, blocks_of[kind], u]) for s in range(2)]
                if not starts(side, kind, u, step):
                    part_copy(side, step - 1, kind, u).wait_recv()
                    come.append((weights[2], arrived[side, step - 1, kind, u]))
                leaving[side, step, kind, u] = mix(kind, come).astype(jnp.bfloat16)
                part_copy(side, step, kind, u).start()

    for u in range(HALF):
        last_step(u)
        merge_step(0, u)
    for step in range(1, steps):
        for u in range(HALF):
            merge_step(step, u)

    source = inverse[me]
    stores = []
    for u in range(HALF):
        for side in SIDES:
            spread_copy(side, steps - 1, u).wait_recv()
            spread_copy(side, steps - 1, u, 1).wait_recv()
        own_weights, _ = weights_of(
            [own_spread(s, source, source, u) for s in range(2)]
            + [arrived_spread[side, steps - 1, u] for side in SIDES]
        )
        other_weights, _ = weights_of([arrived_spread[side, steps, u] for side in SIDES])
        for kind in range(2):
            for side in SIDES:
                part_copy(side, steps - 1, kind, u).wait_recv()
            come = [arrived[side, steps - 1, kind, u] for side in SIDES]
            if kind == 0:
                come = [partials[s, source, u] for s in range(2)] + come
            share = own_weights if kind == 0 else other_weights
            full = mix(kind, zip(share, come)).T.astype(jnp.bfloat16)
            c = HALF * (parity if kind == 0 else 1 - parity) + u
            for j in range(per_chunk):
                merged[c, :, pl.ds(j * HD, HD)] = full[j * rows:(j + 1) * rows]
            store = pltpu.make_async_copy(
                merged.at[c], result.at[:, columns(c)], store_sem.at[2 * u + kind]
            )
            store.start()
            stores.append(store)

    for side in SIDES:
        for u in range(HALF):
            for kind in range(2):
                if goes_on(side, kind, u, steps - 1, steps - 1):
                    gather_copy(side, steps - 1, kind, u, me).wait_send()
                for step in range(steps):
                    if step or kind == 1 or u == side:
                        part_copy(side, step, kind, u).wait_send()
            for step in range(steps):
                spread_copy(side, step, u).wait_send()
            spread_copy(side, steps - 1, u, 1).wait_send()
    for which in range(2):
        for p in range(KV_PIECES):
            kv_copy(which, p).wait_send()
    for store in stores:
        store.wait()


def per_device(queries, cached_keys, cached_values, turn_lengths, tile_map, prefix_len, owner_ids):
    n = lax.axis_size("ctx")
    rows, columns = queries.shape
    cache = cached_keys.shape[0]
    width = columns // CHUNKS
    steps = n // 4
    lanes = rows * width // HD
    hbm = pl.BlockSpec(memory_space=pl.ANY)
    dma = pltpu.SemaphoreType.DMA
    tables = (turn_lengths, tile_map, prefix_len, owner_ids)
    return pl.pallas_call(
        kernel,
        out_shape=jax.ShapeDtypeStruct((rows, columns), jnp.bfloat16),
        in_specs=[hbm] * 7,
        out_specs=hbm,
        scratch_shapes=[pltpu.SMEM(table.shape, jnp.int32) for table in tables]
        + [
            pltpu.SMEM((n,), jnp.int32),
            pltpu.VMEM((HALF, rows, width), jnp.bfloat16),
            pltpu.VMEM((n, HALF, rows, width), jnp.bfloat16),
            pltpu.VMEM((2, n, HALF, HD, lanes), jnp.bfloat16),
            pltpu.VMEM((2, n, HALF, 2, lanes), jnp.float32),
            pltpu.VMEM((2, cache, HD), jnp.bfloat16),
            pltpu.VMEM((2, cache, HD), jnp.bfloat16),
            pltpu.VMEM((2, cache, 2 * HD), jnp.bfloat16),
            pltpu.VMEM((2, HD + COUNT_ROWS, cache), jnp.bfloat16),
            pltpu.VMEM((CHUNKS, rows, width), jnp.bfloat16),
            pltpu.VMEM((2, steps, 2, HALF, HD, lanes), jnp.bfloat16),
            pltpu.VMEM((2, steps, 2, HALF, HD, lanes), jnp.bfloat16),
            pltpu.VMEM((2, steps + 1, HALF, 2, lanes), jnp.float32),
            pltpu.VMEM((2, steps, HALF, 2, lanes), jnp.float32),
            dma((CHUNKS,)),
            dma((len(tables),)),
            dma((2,)),
            dma((2, KV_PIECES)),
            dma((2, KV_PIECES)),
            dma((2, steps, 2, HALF)),
            dma((2, steps, 2, HALF)),
            dma((2, steps, 2, HALF)),
            dma((2, steps, 2, HALF)),
            dma((2, steps + 1, HALF)),
            dma((2, steps + 1, HALF)),
            dma((CHUNKS,)),
        ],
        compiler_params=pltpu.CompilerParams(
            collective_id=0, has_side_effects=True, vmem_limit_bytes=VMEM_BYTES
        ),
        cost_estimate=pl.CostEstimate(
            flops=4 * n * rows * columns * cache,
            bytes_accessed=1 << 20,
            transcendentals=n * rows * columns * cache // HD,
        ),
    )(queries, cached_keys, cached_values, *tables)


VMEM_BYTES = 62 * 1024 * 1024


def solution(mesh):
    return jax.shard_map(
        per_device,
        mesh=mesh,
        in_specs=(
            P(("pack", "ctx"), "head"),
            P(("pack", "ctx"), "head"),
            P(("pack", "ctx"), "head"),
            P("pack"),
            P("pack", None),
            P("pack"),
            P("pack"),
        ),
        out_specs=P(("pack", "ctx"), "head"),
        check_vma=False,
    )
```

time: 279 us -> 70.3 us (0.25)
  waiting for transfers between devices: 146 us -> 0 us
  Pallas kernels: 0 us -> 68.4 us
  starting transfers between devices: 49.8 us -> 0 us
  other arithmetic: 46 us -> 0 us
  matrix products: 18.3 us -> 0 us
  local copies, waits for them, and re-layouts: 15.7 us -> 1.57 us
    ppermute x15 -> x0, waiting for transfers between devices: 74.2 us -> none  [passed_along(): lax.ppermute(x, axis, [(i, (i + by) % length) for i in range(length)])]
    all_to_all x2 -> x0, waiting for transfers between devices: 71.3 us -> none  [the longest x1 60.7 us: per_device(): lax.all_to_all(routed[0].astype(jnp.float32), 'ctx', split_axis=0, concat...]
    pallas_call x0 -> x1, Pallas kernels: none -> 68.4 us  [per_device(): pl.pallas_call(kernel, out_shape=jax.ShapeDtypeStruct((rows, columns), jn...]
    ppermute x15 -> x0, starting transfers between devices: 30.7 us -> none  [passed_along(): lax.ppermute(x, axis, [(i, (i + by) % length) for i in range(length)])]
    reduce_sum x83 -> x0, other arithmetic: 29.5 us -> none  [the longest x32 13.2 us: select_entry(): return jnp.sum(jnp.where(hits, table, 0), axis=table.ndim - 1)]
    all_to_all x2 -> x0, starting transfers between devices: 19.1 us -> none  [the longest x1 9.61 us: per_device(): lax.all_to_all(routed[1], 'ctx', split_axis=0, concat_axis=0, tiled=True)]
    dot_general x32 -> x0, matrix products: 18.3 us -> none  [the longest x16 9.67 us: shard_partial(): jnp.einsum('qgjd,kgd->gjqk', query, key_tiles, preferred_element_type=jnp...]
    lt x16 -> x0, other arithmetic: 8.99 us -> none  [tile_partial(): key_live = lax.iota(jnp.int32, shard_rows) < limit]
  transfers between devices with their start and end apart: 17 -> 0, of which waited for: 17 -> 0; matrix products, arithmetic and copies ran while one was open for 14% -> 0% of each run, Pallas kernels for 0% -> 0%
where the time goes in v2:
time: 70.3 us; the launch traced here: 70 us
  Pallas kernels  68.4 us (97%)
  local copies, waits for them, and re-layouts  1.57 us (2%)
    pallas_call x1, Pallas kernels, per_device(): pl.pallas_call(kernel, out_shape=jax.ShapeDtypeStruct((rows, columns), jn...  68.4 us
    unnamed x1, local copies, waits for them, and re-layouts  1.57 us

profile of v2, /device:TPU:24, one launch (start us, length us, event | category | flops | bytes accessed | tf_op | source)
XLA Modules:
  0.0 70.0 jit_solution(16120232991953529614)
XLA Ops:
  0.0 68.4 %shard_map.73 = bf16[32,2048]{1,0:T(8,128)(2,1)} custom-call(bf16[32,2048]{1,0:T(8,128)(2,1)} %queries.1, bf16[1024,128]{1,0:T(8,128)(2,1)} %cached_keys.1, bf16[1024,128]{1,0:T(8,128)(2,1)} %cached_values.1, s32[8]{0:T(128)} %turn_lengths_in.1, s32[8,16]{1,0:T(8,128)} %tile_map_in.1, s32[16]{0:T(128)} %prefix_len_in.1, s32[16]{0:T(128)} %owner_ids_in.1), custom_call_target="tpu_custom_call" | custom-call | flops 4294967296 | bytes 1048576 | tf_op jit(solution)/shard_map/pallas_call | solution.py:400
  68.4 1.6 %copy.9 = bf16[32,2048]{1,0:T(8,128)(2,1)} copy(bf16[32,2048]{1,0:T(8,128)(2,1)} %shard_map.73) | data formatting | bytes 262144

commit v3 on v2

--- a/solution.py
+++ b/solution.py
@@ -22,10 +22,10 @@
     queries, cached_keys, cached_values, turn_lengths_in, tile_map_in, prefix_len_in, owner_ids_in,
     result,
     turn_lengths, tile_map, prefix_len, owner_ids, inverse,
-    others, blocks, partials, spreads, keys, values, key_rows, value_cols, merged,
+    others, blocks, partials, spreads, keys, values, key_rows, value_cols,
     arrived, leaving, arrived_spread, leaving_spread,
     load_sem, table_sem, kv_load, kv_send, kv_recv, gather_send, gather_recv,
-    part_send, part_recv, spread_send, spread_recv, store_sem,
+    part_send, part_recv, spread_send, spread_recv,
 ):
     n, _, rows, width = blocks.shape
     per_chunk = width // HD
@@ -342,7 +342,6 @@
             merge_step(step, u)
 
     source = inverse[me]
-    stores = []
     for u in range(HALF):
         for side in SIDES:
             spread_copy(side, steps - 1, u).wait_recv()
@@ -362,12 +361,8 @@
             full = mix(kind, zip(share, come)).T.astype(jnp.bfloat16)
             c = HALF * (parity if kind == 0 else 1 - parity) + u
             for j in range(per_chunk):
-                merged[c, :, pl.ds(j * HD, HD)] = full[j * rows:(j + 1) * rows]
-            store = pltpu.make_async_copy(
-                merged.at[c], result.at[:, columns(c)], store_sem.at[2 * u + kind]
-            )
-            store.start()
-            stores.append(store)
+                at = pl.ds(pl.multiple_of(c * width + j * HD, HD), HD)
+                result[:, at] = full[j * rows:(j + 1) * rows]
 
     for side in SIDES:
         for u in range(HALF):
@@ -383,8 +378,6 @@
     for which in range(2):
         for p in range(KV_PIECES):
             kv_copy(which, p).wait_send()
-    for store in stores:
-        store.wait()
 
 
 def per_device(queries, cached_keys, cached_values, turn_lengths, tile_map, prefix_len, owner_ids):
@@ -399,9 +392,9 @@
     tables = (turn_lengths, tile_map, prefix_len, owner_ids)
     return pl.pallas_call(
         kernel,
-        out_shape=jax.ShapeDtypeStruct((rows, columns), jnp.bfloat16),
+        out_shape=pltpu.VMEM((rows, columns), jnp.bfloat16),
         in_specs=[hbm] * 7,
-        out_specs=hbm,
+        out_specs=pl.BlockSpec(memory_space=pltpu.VMEM),
         scratch_shapes=[pltpu.SMEM(table.shape, jnp.int32) for table in tables]
         + [
             pltpu.SMEM((n,), jnp.int32),
@@ -413,7 +406,6 @@
             pltpu.VMEM((2, cache, HD), jnp.bfloat16),
             pltpu.VMEM((2, cache, 2 * HD), jnp.bfloat16),
             pltpu.VMEM((2, HD + COUNT_ROWS, cache), jnp.bfloat16),
-            pltpu.VMEM((CHUNKS, rows, width), jnp.bfloat16),
             pltpu.VMEM((2, steps, 2, HALF, HD, lanes), jnp.bfloat16),
             pltpu.VMEM((2, steps, 2, HALF, HD, lanes), jnp.bfloat16),
             pltpu.VMEM((2, steps + 1, HALF, 2, lanes), jnp.float32),
@@ -429,7 +421,6 @@
             dma((2, steps, 2, HALF)),
             dma((2, steps + 1, HALF)),
             dma((2, steps + 1, HALF)),
-            dma((CHUNKS,)),
         ],
         compiler_params=pltpu.CompilerParams(
             collective_id=0, has_side_effects=True, vmem_limit_bytes=VMEM_BYTES
@@ -439,10 +430,10 @@
             bytes_accessed=1 << 20,
             transcendentals=n * rows * columns * cache // HD,
         ),
-    )(queries, cached_keys, cached_values, *tables)
-
-
-VMEM_BYTES = 62 * 1024 * 1024
+    )(*[pltpu.with_memory_space_constraint(x, pltpu.HBM) for x in (queries, cached_keys, cached_values, *tables)])
+
+
+VMEM_BYTES = 48 * 1024 * 1024
 
 
 def solution(mesh):

time: 70.3 us -> 69 us (0.982)
  local copies, waits for them, and re-layouts: 1.57 us -> 0.66 us
    unnamed x1, local copies, waits for them, and re-layouts: 1.57 us -> 0.66 us
where the time goes in v3:
time: 69 us; the launch traced here: 68.6 us
  Pallas kernels  67.9 us (98%)
    pallas_call x1, Pallas kernels, per_device(): pl.pallas_call(kernel, out_shape=pltpu.VMEM((rows, columns), jnp.bfloat16...  67.9 us

profile of v3, /device:TPU:24, one launch (start us, length us, event | category | flops | bytes accessed | tf_op | source)
XLA Modules:
  0.0 68.6 jit_solution(14328324617051289571)
XLA Ops:
  0.0 67.9 %shard_map.73 = bf16[32,2048]{1,0:T(8,128)(2,1)S(1)} custom-call(bf16[32,2048]{1,0:T(8,128)(2,1)} %queries.1, bf16[1024,128]{1,0:T(8,128)(2,1)} %cached_keys.1, bf16[1024,128]{1,0:T(8,128)(2,1)} %cached_values.1, s32[8]{0:T(128)} %turn_lengths_in.1, s32[8,16]{1,0:T(8,128)} %tile_map_in.1, s32[16]{0:T(128)} %prefix_len_in.1, s32[16]{0:T(128)} %owner_ids_in.1), custom_call_target="tpu_custom_call" | custom-call | flops 4294967296 | bytes 1048576 | tf_op jit(solution)/shard_map/pallas_call | solution.py:393
  67.9 0.7 copy.9

commit v4 on v3

--- a/solution.py
+++ b/solution.py
@@ -53,6 +53,13 @@
     def columns(c):
         return pl.ds(pl.multiple_of(c * width, width), width)
 
+    barrier = pltpu.get_barrier_semaphore()
+    for side in SIDES:
+        for by in (1, 2):
+            pl.semaphore_signal(
+                barrier, inc=1, device_id=device(ahead(side, by)), device_id_type=MESH
+            )
+
     own_loads = [
         pltpu.make_async_copy(
             queries.at[:, columns(HALF * parity + u)], blocks.at[me, u], load_sem.at[u]
@@ -80,15 +87,9 @@
             )
         )
     ]
-    for load in own_loads + other_loads + kv_loads + tables:
+    for load in own_loads + other_loads:
         load.start()
 
-    barrier = pltpu.get_barrier_semaphore()
-    for side in SIDES:
-        for by in (1, 2):
-            pl.semaphore_signal(
-                barrier, inc=1, device_id=device(ahead(side, by)), device_id_type=MESH
-            )
     pl.semaphore_wait(barrier, 4)
 
     def remote(source, target, send_sem, recv_sem, index):
@@ -130,6 +131,8 @@
                 for p in range(KV_PIECES):
                     kv_copy(which, p).start()
 
+    for load in kv_loads + tables:
+        load.start()
     for table in tables:
         table.wait()
     for owner in range(n):
@@ -309,6 +312,7 @@
         return step == 0 or (step == 1 and kind == 0 and u != side)
 
     def merge_step(step, u):
+        blocks_at, shares = [], []
         for side in SIDES:
             far = 2 * (steps - step)
             blocks_of = [inverse[ahead(side, far)], inverse[ahead(side, far - 1)]]
@@ -324,13 +328,16 @@
             spread_copy(side, step, u).start()
             if step == steps - 1:
                 spread_copy(side, step, u, 1).start()
-            for kind in range(2):
+            blocks_at.append(blocks_of)
+            shares.append(weights)
+        for kind in range(2):
+            for side in SIDES:
                 if step == 0 and kind == 0 and u != side:
                     continue
-                come = [(weights[s], partials[s, blocks_of[kind], u]) for s in range(2)]
+                come = [(shares[side][s], partials[s, blocks_at[side][kind], u]) for s in range(2)]
                 if not starts(side, kind, u, step):
                     part_copy(side, step - 1, kind, u).wait_recv()
-                    come.append((weights[2], arrived[side, step - 1, kind, u]))
+                    come.append((shares[side][2], arrived[side, step - 1, kind, u]))
                 leaving[side, step, kind, u] = mix(kind, come).astype(jnp.bfloat16)
                 part_copy(side, step, kind, u).start()
 
@@ -340,6 +347,27 @@
     for step in range(1, steps):
         for u in range(HALF):
             merge_step(step, u)
+
+    def settle(merge_steps):
+        for side in SIDES:
+            for u in range(HALF):
+                for step in merge_steps:
+                    for kind in range(2):
+                        if step or kind == 1 or u == side:
+                            part_copy(side, step, kind, u).wait_send()
+                    spread_copy(side, step, u).wait_send()
+                    if step == steps - 1:
+                        spread_copy(side, step, u, 1).wait_send()
+
+    for side in SIDES:
+        for u in range(HALF):
+            for kind in range(2):
+                if goes_on(side, kind, u, steps - 1, steps - 1):
+                    gather_copy(side, steps - 1, kind, u, me).wait_send()
+    for which in range(2):
+        for p in range(KV_PIECES):
+            kv_copy(which, p).wait_send()
+    settle(range(steps - 1))
 
     source = inverse[me]
     for u in range(HALF):
@@ -364,20 +392,7 @@
                 at = pl.ds(pl.multiple_of(c * width + j * HD, HD), HD)
                 result[:, at] = full[j * rows:(j + 1) * rows]
 
-    for side in SIDES:
-        for u in range(HALF):
-            for kind in range(2):
-                if goes_on(side, kind, u, steps - 1, steps - 1):
-                    gather_copy(side, steps - 1, kind, u, me).wait_send()
-                for step in range(steps):
-                    if step or kind == 1 or u == side:
-                        part_copy(side, step, kind, u).wait_send()
-            for step in range(steps):
-                spread_copy(side, step, u).wait_send()
-            spread_copy(side, steps - 1, u, 1).wait_send()
-    for which in range(2):
-        for p in range(KV_PIECES):
-            kv_copy(which, p).wait_send()
+    settle(range(steps - 1, steps))
 
 
 def per_device(queries, cached_keys, cached_values, turn_lengths, tile_map, prefix_len, owner_ids):

time: 69 us -> 67.4 us (0.977)
  Pallas kernels: 67.9 us -> 66.4 us
    pallas_call x1, Pallas kernels: 67.9 us -> 66.4 us  [per_device(): pl.pallas_call(kernel, out_shape=pltpu.VMEM((rows, columns), jnp.bfloat16...]
where the time goes in v4:
time: 67.4 us; the launch traced here: 67.1 us
  Pallas kernels  66.4 us (99%)
    pallas_call x1, Pallas kernels, per_device(): pl.pallas_call(kernel, out_shape=pltpu.VMEM((rows, columns), jnp.bfloat16...  66.4 us

profile of v4, /device:TPU:24, one launch (start us, length us, event | category | flops | bytes accessed | tf_op | source)
XLA Modules:
  0.0 67.1 jit_solution(6127616454526159906)
XLA Ops:
  0.0 66.4 %shard_map.73 = bf16[32,2048]{1,0:T(8,128)(2,1)S(1)} custom-call(bf16[32,2048]{1,0:T(8,128)(2,1)} %queries.1, bf16[1024,128]{1,0:T(8,128)(2,1)} %cached_keys.1, bf16[1024,128]{1,0:T(8,128)(2,1)} %cached_values.1, s32[8]{0:T(128)} %turn_lengths_in.1, s32[8,16]{1,0:T(8,128)} %tile_map_in.1, s32[16]{0:T(128)} %prefix_len_in.1, s32[16]{0:T(128)} %owner_ids_in.1), custom_call_target="tpu_custom_call" | custom-call | flops 4294967296 | bytes 1048576 | tf_op jit(solution)/shard_map/pallas_call | solution.py:408
  66.4 0.7 copy.9

commit v5 on v4

--- a/solution.py
+++ b/solution.py
@@ -14,7 +14,7 @@
 HALF = CHUNKS // 2
 RIGHT, LEFT = 0, 1
 SIDES = (RIGHT, LEFT)
-KV_PIECES = 4
+KV_PIECES = 2
 COUNT_ROWS = 16
 
 
@@ -232,12 +232,13 @@
     compute((0, own_pairs))
 
     def early_step(it, carry):
-        step, position = it // CHUNKS, lax.rem(it, CHUNKS)
-        arrive(step, position)
-        compute((0, pairs_at(step, position)))
+        step, first = it // HALF, 2 * lax.rem(it, HALF)
+        for position in (first, first + 1):
+            arrive(step, position)
+        compute(*[(0, pairs_at(step, position)) for position in (first, first + 1)])
         return carry
 
-    lax.fori_loop(CHUNKS, 3 * CHUNKS, early_step, 0)
+    lax.fori_loop(HALF, 3 * HALF, early_step, 0)
     for which in range(2):
         for p in range(KV_PIECES):
             kv_copy(which, p).wait_recv()

time: 67.4 us -> 67.5 us (level)
  no operation moved by 1% of the time
where the time goes in v5:
time: 67.5 us; the launch traced here: 66.9 us
  Pallas kernels  66.2 us (98%)
    pallas_call x1, Pallas kernels, per_device(): pl.pallas_call(kernel, out_shape=pltpu.VMEM((rows, columns), jnp.bfloat16...  66.2 us

profile of v5, /device:TPU:24, one launch (start us, length us, event | category | flops | bytes accessed | tf_op | source)
XLA Modules:
  0.0 66.9 jit_solution(11218960115191885401)
XLA Ops:
  0.0 66.2 %shard_map.73 = bf16[32,2048]{1,0:T(8,128)(2,1)S(1)} custom-call(bf16[32,2048]{1,0:T(8,128)(2,1)} %queries.1, bf16[1024,128]{1,0:T(8,128)(2,1)} %cached_keys.1, bf16[1024,128]{1,0:T(8,128)(2,1)} %cached_values.1, s32[8]{0:T(128)} %turn_lengths_in.1, s32[8,16]{1,0:T(8,128)} %tile_map_in.1, s32[16]{0:T(128)} %prefix_len_in.1, s32[16]{0:T(128)} %owner_ids_in.1), custom_call_target="tpu_custom_call" | custom-call | flops 4294967296 | bytes 1048576 | tf_op jit(solution)/shard_map/pallas_call | solution.py:409
  66.2 0.7 copy.9
